TPU v7x, 256 devices: a whole 4x4x8 slice. The times are simulated.
256 devices in a mesh: row: 32 (over z, y), col: 8 (over x, core).
Axes of the slice: x: 4, y: 4, z: 8, core: 2. Of those that a mesh axis runs over, the one named last changes fastest.
Arguments:
- window: float32 [131072, 2048], P('row', 'col'), may hold values from -5 to 5
- outer_diag: float32 [131072], P('row'), may hold values from 0.6 to 1.6
- inner_diag: float32 [131072], P('row'), may hold values from 0.6 to 1.6
- column_diag: float32 [2048], P('col'), may hold values from 0.6 to 1.6
Outputs:
- factored: float32 [131072, 2048], P('row', 'col')
All inputs are finite; a program needn't handle non-finite values.
Results may differ from a plain program's by a relative error of at most 0.000098.
Values sent between devices are 32-bit elements; how exact they have to be, the bound alone decides.
A program may use at most 128 MiB of HBM per device.

v0:
```python
import jax
import jax.numpy as jnp
from jax import lax
from jax.experimental import pallas as pl
from jax.experimental.pallas import tpu as pltpu
from jax.sharding import PartitionSpec as P

MESH = pl.DeviceIdType.MESH
ROOT_HALF = 0.7071067811865476
PANEL = 256
LANES = 128
MEMBERS = 8
CHUNKS = 8
AHEAD = 3
TOP_CHUNKS = CHUNKS // 2
HIGHEST = lax.Precision.HIGHEST


def dot(a, b):
    return jnp.dot(a, b, precision=HIGHEST, preferred_element_type=jnp.float32)


def iota(shape, dim):
    return lax.broadcasted_iota(jnp.int32, shape, dim)


def lu_steps(lu, first, count):
    left = 0 if first < LANES else LANES
    rows, width = PANEL - first, PANEL - left
    lane = iota((1, width), 1) + left
    half_lane = iota((1, LANES), 1) + left
    row_id = iota((rows, 1), 0) + first

    def step(i, carry):
        k = first + i
        pivot_row = lu[pl.ds(k, 1)][:, left:]
        pivot = jnp.sum(jnp.where(half_lane == k, pivot_row[:, :LANES], 0.0), axis=1, keepdims=True)
        column = jnp.sum(
            jnp.where(half_lane == k, lu[first:, left : left + LANES], 0.0), axis=1, keepdims=True
        )
        factor = jnp.where(row_id > k, column / pivot, 0.0)
        lu[first:, left:] = lu[first:, left:] - factor * jnp.where(lane > k, pivot_row, 0.0)
        return carry

    lax.fori_loop(0, count, step, 0)


def invert(lu, unit_upper, low_inv, up_inv):
    i, j = iota((PANEL, PANEL), 0), iota((PANEL, PANEL), 1)
    raw = lu[...]
    diag = jnp.where(i == j, raw, 0.0)
    diag_row = jnp.sum(diag, axis=0, keepdims=True)
    diag_col = jnp.sum(diag, axis=1, keepdims=True)
    lu[...] = jnp.where(i > j, raw / diag_row, raw)
    unit_upper[...] = raw / diag_col
    eye = jnp.where(i == j, 1.0, 0.0)
    low_inv[...] = eye - jnp.where((i == j + 1) & (i % 2 == 1), lu[...], 0.0)
    up_inv[...] = eye - jnp.where((j == i + 1) & (j % 2 == 1), unit_upper[...], 0.0)

    def level(n, carry):
        bi, bj = lax.shift_right_logical(i, n), lax.shift_right_logical(j, n)
        low = jnp.where((bi == bj + 1) & (bi % 2 == 1), lu[...], 0.0)
        up = jnp.where((bj == bi + 1) & (bj % 2 == 1), unit_upper[...], 0.0)
        low_inv[...] -= dot(low_inv[...], dot(low, low_inv[...]))
        up_inv[...] -= dot(up_inv[...], dot(up, up_inv[...]))
        return carry

    lax.fori_loop(1, 8, level, 0)
    up_inv[...] = up_inv[...] / diag_row


def kernel(
    window, outer, inner, cdiag, out,
    d_send, d_recv, d_wide, rx, tx, mixed, panel, result,
    top, a00, lu, unit_upper, low_inv, up_inv, top_out, w,
    s_d, s_rx1, s_tx1, s_rx2, s_tx2, s_prx, s_ptx, s_top, s_aux, s_w, s_wy, s_wtx, s_out,
):
    row, col = lax.axis_index("row"), lax.axis_index("col")
    z, y = row // 4, row % 4
    core = col % 2
    q, xh = row // 8, col // 4
    me = q * 2 + xh
    rows = rx.shape[2]

    def member(mq, mx):
        return (row % 8 + 8 * mq, col % 4 + 4 * mx)

    def remote(src, dst, send, recv, where):
        return pltpu.make_async_remote_copy(src, dst, send, recv, device_id=where, device_id_type=MESH)

    others = [(dq, dx) for dq in range(4) for dx in range(2) if dq or dx]

    def peer(dq, dx):
        return (q + dq) % 4, (xh + dx) % 2

    barrier = pltpu.get_barrier_semaphore()
    partners = [member(*peer(dq, dx)) for dq, dx in others]
    partners += [(row, col // 4 * 4 + (col + n) % 4) for n in range(1, 4)]
    partners += [(row, (col // 4 * 4 + 4) % 8 + (col + n) % 4) for n in range(1, 4)]
    partners += [((z + n) % 8 * 4 + y, col) for n in (1, 3, 5, 7)]
    partners += [(z * 4 + (y + n) % 4, col) for n in range(1, 4)]
    for where in partners:
        pl.semaphore_signal(barrier, inc=1, device_id=where, device_id_type=MESH)
    for p in range(MEMBERS):
        d_send[p, 0:4] = outer[4 * p : 4 * p + 4] * ROOT_HALF
        d_send[p, 4:8] = inner[4 * p : 4 * p + 4] * ROOT_HALF
        d_send[p, 8:10] = cdiag[...] * ROOT_HALF
        d_send[p, 10:16] = jnp.zeros((6, LANES), jnp.float32)
    pl.semaphore_wait(barrier, len(partners))

    pltpu.make_async_copy(d_send.at[me], d_recv.at[me], s_d.at[0]).start()
    for dq, dx in others:
        mq, mx = peer(dq, dx)
        remote(d_send.at[mq * 2 + mx], d_recv.at[me], s_d.at[1], s_d.at[0], member(mq, mx)).start()

    def send_first(k):
        pltpu.make_async_copy(window.at[me, k], rx.at[k, me], s_rx1.at[k]).start()
        for dq, dx in others:
            mq, mx = peer(dq, dx)
            remote(window.at[mq * 2 + mx, k], rx.at[k, me], s_tx1.at[k], s_rx1.at[k], member(mq, mx)).start()

    for k in range(AHEAD):
        send_first(k)

    pltpu.make_async_copy(d_recv, d_recv, s_d.at[0]).wait()
    for n in range(4):
        turned = jnp.transpose(d_recv[2 * n, 0:8])
        for part in range(2):
            for b in range(4):
                lane = 4 * part + b
                d_wide[part * 4 + n, 128 * b : 128 * b + 128] = jnp.broadcast_to(
                    turned[:, lane : lane + 1], (LANES, LANES)
                )

    def mix(k):
        def tile(t, carry):
            r0 = pl.multiple_of(t * 8, 8)
            for h in range(2):
                lanes = slice(h * LANES, h * LANES + LANES)
                od = [d_wide[n, pl.ds(k * rows + r0, 8)] for n in range(4)]
                idg = [d_wide[4 + n, pl.ds(k * rows + r0, 8)] for n in range(4)]
                sides = []
                for side in range(2):
                    x = [rx[k, 2 * n + side, pl.ds(r0, 8), lanes] * od[n] for n in range(4)]
                    a = [x[0] + x[2], x[1] + x[3], x[0] - x[2], x[1] - x[3]]
                    a = [a[n] * idg[n] for n in range(4)]
                    b = [a[0] + a[1], a[0] - a[1], a[2] + a[3], a[2] - a[3]]
                    cd = d_recv[side, 8 + h : 9 + h]
                    sides.append([v * cd for v in b])
                for n in range(4):
                    tx[k, 2 * n, pl.ds(r0, 8), lanes] = sides[0][n] + sides[1][n]
                    tx[k, 2 * n + 1, pl.ds(r0, 8), lanes] = sides[0][n] - sides[1][n]
            return carry

        lax.fori_loop(0, rows // 8, tile, 0)

    def send_second(k, mx):
        for dq in range(4):
            mq = (q + dq) % 4
            src = tx.at[k, mq * 2 + mx]

            def far(src=src, mq=mq):
                remote(src, mixed.at[me, k], s_tx2.at[k], s_rx2.at[k], member(mq, mx)).start()

            if dq:
                far()
            else:
                pl.when(mx != xh)(far)

                @pl.when(mx == xh)
                def _(src=src):
                    pltpu.make_async_copy(src, mixed.at[me, k], s_rx2.at[k]).start()

    half = pl.ds(0, TOP_CHUNKS)

    def tree(src0, src, dst, send, recv, act):
        for column, kids in ((0, ((2, 0), (6, 1), (1, 2))), (2, ((4, 0), (3, 2))), (4, ((5, 2),)), (6, ((7, 2),))):
            @pl.when(col == column)
            def _(column=column, kids=kids):
                for kid, n in kids:
                    act(remote(src0 if column == 0 else src, dst, send.at[n], recv, (row, kid)))

    def start(copy):
        copy.start()

    def wait_send(copy):
        copy.wait_send()

    on_top = row == 0
    for k in range(CHUNKS):
        pltpu.make_async_copy(rx.at[k], rx.at[k], s_rx1.at[k]).wait()
        if k + AHEAD < CHUNKS:
            send_first(k + AHEAD)
        mix(k)
        send_second(k, core)

        if k == TOP_CHUNKS - 1:
            @pl.when(on_top & (col < 4))
            def _():
                remote(tx.at[half, 1], top, s_aux.at[3], s_top.at[0], (row, col + 4)).start()
                pltpu.make_async_copy(tx.at[half, 0], top, s_top.at[0]).start()

            @pl.when(on_top & (col == 0))
            def _():
                pltpu.make_async_copy(tx.at[half, 0], a00, s_top.at[1]).start()
                tree(tx.at[half, 0], a00, a00, s_aux, s_top.at[1], start)

        if k == TOP_CHUNKS:
            @pl.when(on_top)
            def _():
                pltpu.make_async_copy(a00, a00, s_top.at[1]).wait()

                @pl.when(col > 0)
                def _():
                    tree(a00, a00, a00, s_aux, s_top.at[1], start)

                lu[...] = a00[...].reshape(PANEL, PANEL)

        if k >= TOP_CHUNKS:
            @pl.when(on_top)
            def _(k=k):
                lu_steps(lu, 64 * (k - TOP_CHUNKS), 64)

    def send_rest(k, carry):
        send_second(k, 1 - core)
        return carry

    lax.fori_loop(0, CHUNKS, send_rest, 0)

    @pl.when(on_top)
    def _():
        invert(lu, unit_upper, low_inv, up_inv)
        pltpu.make_async_copy(top, top, s_top.at[0]).wait()

        @pl.when(col == 0)
        def _():
            top_out[...] = lu[...]
            w[...] = up_inv[...].reshape(w.shape)

        @pl.when(col > 0)
        def _():
            top_out[...] = dot(low_inv[...], top[...].reshape(PANEL, PANEL))
            w[...] = dot(up_inv[...], top_out[...]).reshape(w.shape)

    def w_scatter(act):
        @pl.when(on_top)
        def _():
            for n in range(1, 4):
                act(remote(w.at[n], w.at[n], s_wtx.at[n - 1], s_w, (n, col)))

    def w_along_z(act):
        @pl.when(z == 0)
        def _():
            for n in range(1, 8):
                act(remote(w.at[y], w.at[y], s_wtx.at[2 + n], s_w, (n * 4 + y, col)))

    def w_along_y(act):
        for n in range(1, 4):
            @pl.when((z > 0) | (y != 4 - n))
            def _(n=n):
                act(remote(w.at[y], w.at[y], s_wtx.at[9 + n], s_wy.at[n - 1], (z * 4 + (y + n) % 4, col)))

    @pl.when(on_top)
    def _():
        w_scatter(start)
        w_along_z(start)
        w_along_y(start)

    def relay(k, carry):
        @pl.when(col == 0)
        def _():
            pltpu.make_async_copy(mixed.at[:, k], mixed.at[:, k], s_rx2.at[k]).wait()

        @pl.when(col > 0)
        def _():
            pltpu.make_async_copy(panel.at[:, k], panel.at[:, k], s_prx.at[k]).wait()

        tree(mixed.at[:, k], panel.at[:, k], panel.at[:, k], s_ptx.at[k], s_prx.at[k], start)
        return carry

    lax.fori_loop(0, CHUNKS, relay, 0)

    @pl.when(row > 0)
    def _():
        pltpu.make_async_copy(w.at[y], w.at[y], s_w).wait()
        w_along_z(start)
        w_along_y(start)
        for n in range(1, 4):
            pltpu.make_async_copy(w.at[0], w.at[0], s_wy.at[n - 1]).wait()

    def finish(k, carry):
        @pl.when(col == 0)
        def _():
            whole = mixed[:, k].reshape(MEMBERS * rows, PANEL)
            result[:, k] = dot(whole, w[...].reshape(PANEL, PANEL)).reshape(MEMBERS, rows, PANEL)

        @pl.when(col > 0)
        def _():
            whole = panel[:, k].reshape(MEMBERS * rows, PANEL)
            product = dot(whole, w[...].reshape(PANEL, PANEL)).reshape(MEMBERS, rows, PANEL)
            pltpu.make_async_copy(mixed.at[:, k], mixed.at[:, k], s_rx2.at[k]).wait()
            result[:, k] = mixed[:, k] - product

        @pl.when(on_top & (k < TOP_CHUNKS))
        def _():
            result[0, k] = top_out[pl.ds(pl.multiple_of(k * rows, rows), rows)]

        pltpu.make_async_copy(result.at[:, k], out.at[:, k], s_out.at[k]).start()
        return carry

    lax.fori_loop(0, CHUNKS, finish, 0)

    seven = pl.ds(0, 7)

    def drain(k, carry):
        pltpu.make_async_copy(rx.at[k, seven], rx.at[k, seven], s_tx1.at[k]).wait()
        pltpu.make_async_copy(tx.at[k, seven], tx.at[k, seven], s_tx2.at[k]).wait()
        tree(mixed.at[:, k], panel.at[:, k], panel.at[:, k], s_ptx.at[k], s_prx.at[k], wait_send)
        pltpu.make_async_copy(result.at[:, k], out.at[:, k], s_out.at[k]).wait()
        return carry

    lax.fori_loop(0, CHUNKS, drain, 0)
    pltpu.make_async_copy(d_recv.at[seven], d_recv.at[seven], s_d.at[1]).wait()

    @pl.when(on_top & (col < 4))
    def _():
        remote(tx.at[half, 1], top, s_aux.at[3], s_top.at[0], (row, col + 4)).wait_send()

    @pl.when(on_top)
    def _():
        tree(tx.at[half, 0], a00, a00, s_aux, s_top.at[1], wait_send)

    w_scatter(wait_send)
    w_along_z(wait_send)
    w_along_y(wait_send)


def local(window, outer_diag, inner_diag, column_diag):
    local_rows, local_cols = window.shape
    rows = local_rows // (MEMBERS * CHUNKS)
    pieces = (MEMBERS, CHUNKS, rows, local_cols)
    f32 = jnp.float32
    dma = pltpu.SemaphoreType.DMA
    square = pltpu.VMEM((PANEL, PANEL), f32)
    quarters = pltpu.VMEM((4, PANEL // 4, PANEL), f32)
    vmem = pl.BlockSpec(memory_space=pltpu.VMEM)
    anywhere = pl.BlockSpec(memory_space=pl.ANY)
    factored = pl.pallas_call(
        kernel,
        out_shape=jax.ShapeDtypeStruct(pieces, f32),
        in_specs=[anywhere, vmem, vmem, vmem],
        out_specs=anywhere,
        scratch_shapes=[
            pltpu.VMEM((MEMBERS, 16, LANES), f32),
            pltpu.VMEM((MEMBERS, 16, LANES), f32),
            pltpu.VMEM((8, local_rows // MEMBERS, LANES), f32),
            pltpu.VMEM((CHUNKS, MEMBERS, rows, local_cols), f32),
            pltpu.VMEM((CHUNKS, MEMBERS, rows, local_cols), f32),
            pltpu.VMEM(pieces, f32),
            pltpu.VMEM(pieces, f32),
            pltpu.VMEM(pieces, f32),
            quarters,
            quarters,
            square,
            square,
            square,
            square,
            square,
            quarters,
            dma((2,)),
            dma((CHUNKS,)),
            dma((CHUNKS,)),
            dma((CHUNKS,)),
            dma((CHUNKS,)),
            dma((CHUNKS,)),
            dma((CHUNKS, 3)),
            dma((2,)),
            dma((4,)),
            dma,
            dma((3,)),
            dma((13,)),
            dma((CHUNKS,)),
        ],
        compiler_params=pltpu.CompilerParams(
            collective_id=0, has_side_effects=True, vmem_limit_bytes=48 * 2**20
        ),
        name="butterfly_lu",
    )(
        window.reshape(pieces),
        outer_diag.reshape(local_rows // LANES, LANES),
        inner_diag.reshape(local_rows // LANES, LANES),
        column_diag.reshape(local_cols // LANES, LANES),
    )
    return factored.reshape(local_rows, local_cols)


def solution(mesh):
    in_specs = (P("row", "col"), P("row"), P("row"), P("col"))
    return jax.shard_map(
        local, mesh=mesh, in_specs=in_specs, out_specs=P("row", "col"), check_vma=False
    )
```

profile of v0, /device:TPU:37, one launch (start us, length us, event | category | flops | bytes accessed | tf_op | source)
XLA Modules:
  0.0 273.2 jit_solution(17619609214053550691)
XLA Ops:
  0.0 0.0 copy-start
  0.0 0.7 copy-done
  0.7 0.0 copy-start.1
  0.7 0.7 copy-done.1
  1.4 0.0 copy-start.2
  1.4 0.7 copy-done.2
  2.1 269.1 %butterfly_lu.1 = f32[8,8,64,256]{3,2,1,0:T(8,128)S(1)} custom-call(f32[8,8,64,256]{3,2,1,0:T(8,128)} %bitcast.9, f32[32,128]{1,0:T(8,128)S(1)} %bitcast.6, f32[32,128]{1,0:T(8,128)S(1)} %bitcast.7, f32[2,128]{1,0:T(2,128)S(1)} %bitcast.8), custom_call_target="tpu_custom_call" | custom-call | tf_op jit(solution)/shard_map/butterfly_lu/pallas_call | solution.py:348
  271.2 2.0 copy.6
Async XLA Ops:
  0.0 0.7 copy-start
  0.7 0.7 copy-start.1
  1.4 0.7 copy-start.2
where the time goes:
time: 273 us
  Pallas kernels  269 us (99%)
  local copies, waits for them, and re-layouts  4.13 us (2%)
    pallas_call x1, Pallas kernels, local(): pl.pallas_call(kernel, out_shape=jax.ShapeDtypeStruct(pieces, f32), in_sp...  269 us

commit v1 on v0

--- a/solution.py
+++ b/solution.py
@@ -11,7 +11,7 @@
 LANES = 128
 MEMBERS = 8
 CHUNKS = 8
-AHEAD = 3
+AHEAD = 8
 TOP_CHUNKS = CHUNKS // 2
 HIGHEST = lax.Precision.HIGHEST
 

time: 273 us -> 225 us (0.82)
  the two profiles are of different devices: /device:TPU:37 before, /device:TPU:149 now
where the time goes in v1:
time: 225 us
  Pallas kernels  221 us (98%)
  local copies, waits for them, and re-layouts  4.13 us (2%)
    pallas_call x1, Pallas kernels, local(): pl.pallas_call(kernel, out_shape=jax.ShapeDtypeStruct(pieces, f32), in_sp...  221 us

profile of v1, /device:TPU:149, one launch (start us, length us, event | category | flops | bytes accessed | tf_op | source)
XLA Modules:
  0.0 225.1 jit_solution(2337693626207546739)
XLA Ops:
  0.0 0.0 copy-start
  0.0 0.7 copy-done
  0.7 0.0 copy-start.1
  0.7 0.7 copy-done.1
  1.4 0.0 copy-start.2
  1.4 0.7 copy-done.2
  2.1 221.0 %butterfly_lu.1 = f32[8,8,64,256]{3,2,1,0:T(8,128)S(1)} custom-call(f32[8,8,64,256]{3,2,1,0:T(8,128)} %bitcast.9, f32[32,128]{1,0:T(8,128)S(1)} %bitcast.6, f32[32,128]{1,0:T(8,128)S(1)} %bitcast.7, f32[2,128]{1,0:T(2,128)S(1)} %bitcast.8), custom_call_target="tpu_custom_call" | custom-call | tf_op jit(solution)/shard_map/butterfly_lu/pallas_call | solution.py:348
  223.1 2.0 copy.6
Async XLA Ops:
  0.0 0.7 copy-start
  0.7 0.7 copy-start.1
  1.4 0.7 copy-start.2

commit v2 on v1

--- a/solution.py
+++ b/solution.py
@@ -11,7 +11,7 @@
 LANES = 128
 MEMBERS = 8
 CHUNKS = 8
-AHEAD = 8
+W_AT = 4
 TOP_CHUNKS = CHUNKS // 2
 HIGHEST = lax.Precision.HIGHEST
 
@@ -70,10 +70,10 @@
 
 
 def kernel(
-    window, outer, inner, cdiag, out,
-    d_send, d_recv, d_wide, rx, tx, mixed, panel, result,
+    window, outer_hbm, inner_hbm, cdiag_hbm, out,
+    outer, inner, cdiag, d_send, d_recv, d_wide, rx, tx, mixed, panel, result,
     top, a00, lu, unit_upper, low_inv, up_inv, top_out, w,
-    s_d, s_rx1, s_tx1, s_rx2, s_tx2, s_prx, s_ptx, s_top, s_aux, s_w, s_wy, s_wtx, s_out,
+    s_d, s_rx1, s_tx1, s_rx2, s_tx2, s_pa, s_pb, s_ptx, s_top, s_aux, s_w, s_wy, s_wtx, s_out, s_in,
 ):
     row, col = lax.axis_index("row"), lax.axis_index("col")
     z, y = row // 4, row % 4
@@ -90,8 +90,18 @@
 
     others = [(dq, dx) for dq in range(4) for dx in range(2) if dq or dx]
 
+    def turned_q(dq):
+        return (q, q + 1 - 2 * (q % 2), (q + 2) % 4, 3 - q)[dq]
+
     def peer(dq, dx):
-        return (q + dq) % 4, (xh + dx) % 2
+        return turned_q(dq), (xh + dx) % 2
+
+    loads = [
+        pltpu.make_async_copy(src, dst, s_in.at[n])
+        for n, (src, dst) in enumerate(((outer_hbm, outer), (inner_hbm, inner), (cdiag_hbm, cdiag)))
+    ]
+    for load in loads:
+        load.start()
 
     barrier = pltpu.get_barrier_semaphore()
     partners = [member(*peer(dq, dx)) for dq, dx in others]
@@ -101,6 +111,8 @@
     partners += [(z * 4 + (y + n) % 4, col) for n in range(1, 4)]
     for where in partners:
         pl.semaphore_signal(barrier, inc=1, device_id=where, device_id_type=MESH)
+    for load in loads:
+        load.wait()
     for p in range(MEMBERS):
         d_send[p, 0:4] = outer[4 * p : 4 * p + 4] * ROOT_HALF
         d_send[p, 4:8] = inner[4 * p : 4 * p + 4] * ROOT_HALF
@@ -114,12 +126,12 @@
         remote(d_send.at[mq * 2 + mx], d_recv.at[me], s_d.at[1], s_d.at[0], member(mq, mx)).start()
 
     def send_first(k):
-        pltpu.make_async_copy(window.at[me, k], rx.at[k, me], s_rx1.at[k]).start()
+        pltpu.make_async_copy(window.at[q, xh, k], rx.at[k, me], s_rx1.at[k]).start()
         for dq, dx in others:
             mq, mx = peer(dq, dx)
-            remote(window.at[mq * 2 + mx, k], rx.at[k, me], s_tx1.at[k], s_rx1.at[k], member(mq, mx)).start()
-
-    for k in range(AHEAD):
+            remote(window.at[mq, mx, k], rx.at[k, me], s_tx1.at[k], s_rx1.at[k], member(mq, mx)).start()
+
+    for k in range(CHUNKS):
         send_first(k)
 
     pltpu.make_async_copy(d_recv, d_recv, s_d.at[0]).wait()
@@ -154,31 +166,42 @@
 
         lax.fori_loop(0, rows // 8, tile, 0)
 
+    panel_group = col % 4 == 0
+
     def send_second(k, mx):
+        here = panel_group & (xh == 1) & (mx == 0)
         for dq in range(4):
-            mq = (q + dq) % 4
+            mq = turned_q(dq)
             src = tx.at[k, mq * 2 + mx]
 
             def far(src=src, mq=mq):
-                remote(src, mixed.at[me, k], s_tx2.at[k], s_rx2.at[k], member(mq, mx)).start()
+                remote(src, mixed.at[q, xh, k], s_tx2.at[k], s_rx2.at[k], member(mq, mx)).start()
+
+            def near(src=src, mq=mq):
+                remote(src, panel.at[q, xh, k], s_tx2.at[k], s_pb.at[k], member(mq, 1)).start()
 
             if dq:
-                far()
+                pl.when(here)(near)
+                pl.when(jnp.logical_not(here))(far)
             else:
-                pl.when(mx != xh)(far)
+                pl.when((mx != xh) & jnp.logical_not(here))(far)
+
+                @pl.when(here)
+                def _(src=src):
+                    pltpu.make_async_copy(src, panel.at[q, xh, k], s_pb.at[k]).start()
 
                 @pl.when(mx == xh)
                 def _(src=src):
-                    pltpu.make_async_copy(src, mixed.at[me, k], s_rx2.at[k]).start()
+                    pltpu.make_async_copy(src, mixed.at[q, xh, k], s_rx2.at[k]).start()
 
     half = pl.ds(0, TOP_CHUNKS)
 
-    def tree(src0, src, dst, send, recv, act):
-        for column, kids in ((0, ((2, 0), (6, 1), (1, 2))), (2, ((4, 0), (3, 2))), (4, ((5, 2),)), (6, ((7, 2),))):
+    def spread_a00(src0, act):
+        for column, kids in ((0, (4, 2, 6, 1)), (2, (3,)), (4, (5,)), (6, (7,))):
             @pl.when(col == column)
             def _(column=column, kids=kids):
-                for kid, n in kids:
-                    act(remote(src0 if column == 0 else src, dst, send.at[n], recv, (row, kid)))
+                for n, kid in enumerate(kids):
+                    act(remote(src0 if column == 0 else a00, a00, s_aux.at[n], s_top.at[1], (row, kid)))
 
     def start(copy):
         copy.start()
@@ -187,49 +210,17 @@
         copy.wait_send()
 
     on_top = row == 0
-    for k in range(CHUNKS):
-        pltpu.make_async_copy(rx.at[k], rx.at[k], s_rx1.at[k]).wait()
-        if k + AHEAD < CHUNKS:
-            send_first(k + AHEAD)
-        mix(k)
-        send_second(k, core)
-
-        if k == TOP_CHUNKS - 1:
-            @pl.when(on_top & (col < 4))
-            def _():
-                remote(tx.at[half, 1], top, s_aux.at[3], s_top.at[0], (row, col + 4)).start()
-                pltpu.make_async_copy(tx.at[half, 0], top, s_top.at[0]).start()
-
-            @pl.when(on_top & (col == 0))
-            def _():
-                pltpu.make_async_copy(tx.at[half, 0], a00, s_top.at[1]).start()
-                tree(tx.at[half, 0], a00, a00, s_aux, s_top.at[1], start)
-
-        if k == TOP_CHUNKS:
-            @pl.when(on_top)
-            def _():
-                pltpu.make_async_copy(a00, a00, s_top.at[1]).wait()
-
-                @pl.when(col > 0)
-                def _():
-                    tree(a00, a00, a00, s_aux, s_top.at[1], start)
-
-                lu[...] = a00[...].reshape(PANEL, PANEL)
-
-        if k >= TOP_CHUNKS:
-            @pl.when(on_top)
-            def _(k=k):
-                lu_steps(lu, 64 * (k - TOP_CHUNKS), 64)
-
-    def send_rest(k, carry):
-        send_second(k, 1 - core)
-        return carry
-
-    lax.fori_loop(0, CHUNKS, send_rest, 0)
-
-    @pl.when(on_top)
-    def _():
-        invert(lu, unit_upper, low_inv, up_inv)
+
+    def take_a00():
+        pltpu.make_async_copy(a00, a00, s_top.at[1]).wait()
+
+        @pl.when(col > 0)
+        def _():
+            spread_a00(a00, start)
+
+        lu[...] = a00[...].reshape(PANEL, PANEL)
+
+    def solve_top():
         pltpu.make_async_copy(top, top, s_top.at[0]).wait()
 
         @pl.when(col == 0)
@@ -260,63 +251,188 @@
             def _(n=n):
                 act(remote(w.at[y], w.at[y], s_wtx.at[9 + n], s_wy.at[n - 1], (z * 4 + (y + n) % 4, col)))
 
-    @pl.when(on_top)
-    def _():
+    def top_rows():
+        @pl.when(on_top & (col < 4))
+        def _():
+            remote(tx.at[half, 1], top, s_aux.at[4], s_top.at[0], (row, col + 4)).start()
+            pltpu.make_async_copy(tx.at[half, 0], top, s_top.at[0]).start()
+
+        @pl.when(on_top & (col == 0))
+        def _():
+            pltpu.make_async_copy(tx.at[half, 0], a00, s_top.at[1]).start()
+            spread_a00(tx.at[half, 0], start)
+
+    def w_from_top():
+        invert(lu, unit_upper, low_inv, up_inv)
+        solve_top()
         w_scatter(start)
         w_along_z(start)
         w_along_y(start)
 
-    def relay(k, carry):
-        @pl.when(col == 0)
-        def _():
-            pltpu.make_async_copy(mixed.at[:, k], mixed.at[:, k], s_rx2.at[k]).wait()
-
-        @pl.when(col > 0)
-        def _():
-            pltpu.make_async_copy(panel.at[:, k], panel.at[:, k], s_prx.at[k]).wait()
-
-        tree(mixed.at[:, k], panel.at[:, k], panel.at[:, k], s_ptx.at[k], s_prx.at[k], start)
-        return carry
-
-    lax.fori_loop(0, CHUNKS, relay, 0)
+    def w_onward():
+        @pl.when(row > 0)
+        def _():
+            pltpu.make_async_copy(w.at[y], w.at[y], s_w).wait()
+            w_along_z(start)
+            w_along_y(start)
+
+    def even_of(ref, k):
+        return ref.at[:, 0, k]
+
+    def odd_of(ref, k):
+        return ref.at[:, 1, k]
+
+    def panel_even(column, k):
+        src = even_of(mixed if column == 0 else panel, k)
+        kids = {0: (2, 6, 1), 2: (3, 4)[: 2 - k % 2], 4: (5,), 6: (7, 4)[: 1 + k % 2]}[column]
+        return [remote(src, even_of(panel, k), s_ptx.at[k, n], s_pa.at[k], (row, kid)) for n, kid in enumerate(kids)]
+
+    def panel_odd(column, k):
+        src = odd_of(mixed if column == 0 else panel, k)
+        kids = {0: (1,), 2: (3, 0)[: 2 - k % 2], 4: (2, 6, 5), 6: (7, 0)[: 1 + k % 2]}[column]
+        return [
+            remote(src, odd_of(mixed if kid == 0 else panel, k), s_ptx.at[k, 4 + n], s_pb.at[k], (row, kid))
+            for n, kid in enumerate(kids)
+        ]
+
+    def await_even(k):
+        pltpu.make_async_copy(even_of(panel, k), even_of(panel, k), s_pa.at[k]).wait()
+
+    def await_odd(k):
+        pltpu.make_async_copy(odd_of(panel, k), odd_of(panel, k), s_pb.at[k]).wait()
+
+    def send_even(column, k):
+        for copy in panel_even(column, k):
+            copy.start()
+
+    def send_odd(column, k):
+        for copy in panel_odd(column, k):
+            copy.start()
+
+    def send_slab(mx):
+        def body(k, carry):
+            send_second(k, mx)
+            return carry
+
+        lax.fori_loop(0, CHUNKS, body, 0)
+
+    for k in range(CHUNKS):
+        pltpu.make_async_copy(rx.at[k], rx.at[k], s_rx1.at[k]).wait()
+        mix(k)
+        send_second(k, core)
+        if k == TOP_CHUNKS - 1:
+            top_rows()
+        if k == TOP_CHUNKS:
+            pl.when(on_top)(take_a00)
+        if k >= TOP_CHUNKS:
+            @pl.when(on_top)
+            def _(k=k):
+                lu_steps(lu, 64 * (k - TOP_CHUNKS), 64)
+
+    pl.when(on_top)(w_from_top)
+    @pl.when(col == 0)
+    def _():
+        for k in range(CHUNKS):
+            if k == W_AT:
+                pl.when(z == 0)(w_onward)
+            pltpu.make_async_copy(even_of(mixed, k), even_of(mixed, k), s_rx2.at[k]).wait()
+            send_even(0, k)
+            send_second(k, 1)
+        for k in range(CHUNKS):
+            await_odd(k)
+            send_odd(0, k)
+
+    @pl.when(col == 4)
+    def _():
+        for k in range(CHUNKS):
+            if k == W_AT:
+                pl.when(z == 0)(w_onward)
+            await_odd(k)
+            send_odd(4, k)
+            send_second(k, 1)
+        for k in range(CHUNKS):
+            await_even(k)
+            send_even(4, k)
+
+    for column in (2, 6):
+        @pl.when(col == column)
+        def _(column=column):
+            for k in range(CHUNKS):
+                if k == W_AT:
+                    pl.when(z == 0)(w_onward)
+                await_even(k)
+                send_even(column, k)
+                await_odd(k)
+                send_odd(column, k)
+                send_second(k, 1)
+
+    @pl.when(core == 1)
+    def _():
+        pl.when(z == 0)(w_onward)
+        send_slab(0)
+        for k in range(CHUNKS):
+            await_even(k)
+            await_odd(k)
+
+    pl.when(z > 0)(w_onward)
 
     @pl.when(row > 0)
     def _():
-        pltpu.make_async_copy(w.at[y], w.at[y], s_w).wait()
-        w_along_z(start)
-        w_along_y(start)
         for n in range(1, 4):
             pltpu.make_async_copy(w.at[0], w.at[0], s_wy.at[n - 1]).wait()
 
+    def multiply(k, carry):
+        def product(ref):
+            whole = ref[:, :, k].reshape(MEMBERS * rows, PANEL)
+            return dot(whole, w[...].reshape(PANEL, PANEL)).reshape(4, 2, rows, PANEL)
+
+        @pl.when(col == 0)
+        def _():
+            result[:, :, k] = product(mixed)
+
+        @pl.when(col > 0)
+        def _():
+            result[:, :, k] = product(panel)
+
+        return carry
+
+    lax.fori_loop(0, CHUNKS, multiply, 0)
+
     def finish(k, carry):
-        @pl.when(col == 0)
-        def _():
-            whole = mixed[:, k].reshape(MEMBERS * rows, PANEL)
-            result[:, k] = dot(whole, w[...].reshape(PANEL, PANEL)).reshape(MEMBERS, rows, PANEL)
-
         @pl.when(col > 0)
         def _():
-            whole = panel[:, k].reshape(MEMBERS * rows, PANEL)
-            product = dot(whole, w[...].reshape(PANEL, PANEL)).reshape(MEMBERS, rows, PANEL)
-            pltpu.make_async_copy(mixed.at[:, k], mixed.at[:, k], s_rx2.at[k]).wait()
-            result[:, k] = mixed[:, k] - product
+            pltpu.make_async_copy(mixed.at[:, :, k], mixed.at[:, :, k], s_rx2.at[k]).wait()
+            result[:, :, k] = mixed[:, :, k] - result[:, :, k]
 
         @pl.when(on_top & (k < TOP_CHUNKS))
         def _():
-            result[0, k] = top_out[pl.ds(pl.multiple_of(k * rows, rows), rows)]
-
-        pltpu.make_async_copy(result.at[:, k], out.at[:, k], s_out.at[k]).start()
+            result[0, 0, k] = top_out[pl.ds(pl.multiple_of(k * rows, rows), rows)]
+
+        pltpu.make_async_copy(result.at[:, :, k], out.at[:, :, k], s_out.at[k]).start()
         return carry
 
     lax.fori_loop(0, CHUNKS, finish, 0)
+
+    for column in (0, 2, 4, 6):
+        @pl.when(col == column)
+        def _(column=column):
+            for k in range(CHUNKS):
+                for copy in panel_even(column, k) + panel_odd(column, k):
+                    copy.wait_send()
 
     seven = pl.ds(0, 7)
 
     def drain(k, carry):
         pltpu.make_async_copy(rx.at[k, seven], rx.at[k, seven], s_tx1.at[k]).wait()
-        pltpu.make_async_copy(tx.at[k, seven], tx.at[k, seven], s_tx2.at[k]).wait()
-        tree(mixed.at[:, k], panel.at[:, k], panel.at[:, k], s_ptx.at[k], s_prx.at[k], wait_send)
-        pltpu.make_async_copy(result.at[:, k], out.at[:, k], s_out.at[k]).wait()
+        @pl.when(col != 4)
+        def _():
+            pltpu.make_async_copy(tx.at[k, seven], tx.at[k, seven], s_tx2.at[k]).wait()
+
+        @pl.when(col == 4)
+        def _():
+            pltpu.make_async_copy(tx.at[k, pl.ds(0, 6)], tx.at[k, pl.ds(0, 6)], s_tx2.at[k]).wait()
+
+        pltpu.make_async_copy(result.at[:, :, k], out.at[:, :, k], s_out.at[k]).wait()
         return carry
 
     lax.fori_loop(0, CHUNKS, drain, 0)
@@ -324,11 +440,11 @@
 
     @pl.when(on_top & (col < 4))
     def _():
-        remote(tx.at[half, 1], top, s_aux.at[3], s_top.at[0], (row, col + 4)).wait_send()
+        remote(tx.at[half, 1], top, s_aux.at[4], s_top.at[0], (row, col + 4)).wait_send()
 
     @pl.when(on_top)
     def _():
-        tree(tx.at[half, 0], a00, a00, s_aux, s_top.at[1], wait_send)
+        spread_a00(tx.at[half, 0], wait_send)
 
     w_scatter(wait_send)
     w_along_z(wait_send)
@@ -338,19 +454,21 @@
 def local(window, outer_diag, inner_diag, column_diag):
     local_rows, local_cols = window.shape
     rows = local_rows // (MEMBERS * CHUNKS)
-    pieces = (MEMBERS, CHUNKS, rows, local_cols)
+    pieces = (4, 2, CHUNKS, rows, local_cols)
     f32 = jnp.float32
     dma = pltpu.SemaphoreType.DMA
     square = pltpu.VMEM((PANEL, PANEL), f32)
     quarters = pltpu.VMEM((4, PANEL // 4, PANEL), f32)
-    vmem = pl.BlockSpec(memory_space=pltpu.VMEM)
     anywhere = pl.BlockSpec(memory_space=pl.ANY)
     factored = pl.pallas_call(
         kernel,
         out_shape=jax.ShapeDtypeStruct(pieces, f32),
-        in_specs=[anywhere, vmem, vmem, vmem],
+        in_specs=[anywhere] * 4,
         out_specs=anywhere,
         scratch_shapes=[
+            pltpu.VMEM((local_rows // LANES, LANES), f32),
+            pltpu.VMEM((local_rows // LANES, LANES), f32),
+            pltpu.VMEM((local_cols // LANES, LANES), f32),
             pltpu.VMEM((MEMBERS, 16, LANES), f32),
             pltpu.VMEM((MEMBERS, 16, LANES), f32),
             pltpu.VMEM((8, local_rows // MEMBERS, LANES), f32),
@@ -373,13 +491,15 @@
             dma((CHUNKS,)),
             dma((CHUNKS,)),
             dma((CHUNKS,)),
-            dma((CHUNKS, 3)),
+            dma((CHUNKS,)),
+            dma((CHUNKS, 8)),
             dma((2,)),
-            dma((4,)),
+            dma((5,)),
             dma,
             dma((3,)),
             dma((13,)),
             dma((CHUNKS,)),
+            dma((3,)),
         ],
         compiler_params=pltpu.CompilerParams(
             collective_id=0, has_side_effects=True, vmem_limit_bytes=48 * 2**20

time: 225 us -> 219 us (0.973)
  the two profiles are of different devices: /device:TPU:149 before, /device:TPU:65 now
where the time goes in v2:
time: 219 us
  Pallas kernels  214 us (98%)
  local copies, waits for them, and re-layouts  4.13 us (2%)
    pallas_call x1, Pallas kernels, local(): pl.pallas_call(kernel, out_shape=jax.ShapeDtypeStruct(pieces, f32), in_sp...  214 us

profile of v2, /device:TPU:65, one launch (start us, length us, event | category | flops | bytes accessed | tf_op | source)
XLA Modules:
  0.0 218.5 jit_solution(6857570008766594350)
XLA Ops:
  0.0 0.0 copy-start
  0.0 0.7 copy-done
  0.7 0.0 copy-start.1
  0.7 0.7 copy-done.1
  1.4 0.0 copy-start.2
  1.4 0.7 copy-done.2
  2.1 214.4 %butterfly_lu.1 = f32[4,2,8,64,256]{4,3,2,1,0:T(8,128)S(1)} custom-call(f32[4,2,8,64,256]{4,3,2,1,0:T(8,128)} %bitcast.9, f32[32,128]{1,0:T(8,128)S(1)} %bitcast.6, f32[32,128]{1,0:T(8,128)S(1)} %bitcast.7, f32[2,128]{1,0:T(2,128)S(1)} %bitcast.8), custom_call_target="tpu_custom_call" | custom-call | tf_op jit(solution)/shard_map/butterfly_lu/pallas_call | solution.py:463
  216.5 2.0 copy.6
Async XLA Ops:
  0.0 0.7 copy-start
  0.7 0.7 copy-start.1
  1.4 0.7 copy-start.2

commit v3 on v2

--- a/solution.py
+++ b/solution.py
@@ -11,7 +11,7 @@
 LANES = 128
 MEMBERS = 8
 CHUNKS = 8
-W_AT = 4
+W_AT = 7
 TOP_CHUNKS = CHUNKS // 2
 HIGHEST = lax.Precision.HIGHEST
 
@@ -368,8 +368,10 @@
 
     @pl.when(core == 1)
     def _():
-        pl.when(z == 0)(w_onward)
-        send_slab(0)
+        for k in range(CHUNKS):
+            if k == 6:
+                pl.when(z == 0)(w_onward)
+            send_second(k, 0)
         for k in range(CHUNKS):
             await_even(k)
             await_odd(k)

time: 219 us -> 216 us (0.986)
  Pallas kernels: 214 us -> 211 us
    pallas_call x1, Pallas kernels: 214 us -> 211 us  [local(): pl.pallas_call(kernel, out_shape=jax.ShapeDtypeStruct(pieces, f32), in_sp...]
where the time goes in v3:
time: 216 us; the launch traced here: 215 us
  Pallas kernels  211 us (98%)
  local copies, waits for them, and re-layouts  4.13 us (2%)
    pallas_call x1, Pallas kernels, local(): pl.pallas_call(kernel, out_shape=jax.ShapeDtypeStruct(pieces, f32), in_sp...  211 us

profile of v3, /device:TPU:65, one launch (start us, length us, event | category | flops | bytes accessed | tf_op | source)
XLA Modules:
  0.0 215.3 jit_solution(3624089873779201149)
XLA Ops:
  0.0 0.0 copy-start
  0.0 0.7 copy-done
  0.7 0.0 copy-start.1
  0.7 0.7 copy-done.1
  1.4 0.0 copy-start.2
  1.4 0.7 copy-done.2
  2.1 211.1 %butterfly_lu.1 = f32[4,2,8,64,256]{4,3,2,1,0:T(8,128)S(1)} custom-call(f32[4,2,8,64,256]{4,3,2,1,0:T(8,128)} %bitcast.9, f32[32,128]{1,0:T(8,128)S(1)} %bitcast.6, f32[32,128]{1,0:T(8,128)S(1)} %bitcast.7, f32[2,128]{1,0:T(2,128)S(1)} %bitcast.8), custom_call_target="tpu_custom_call" | custom-call | tf_op jit(solution)/shard_map/butterfly_lu/pallas_call | solution.py:465
  213.3 2.0 copy.6
Async XLA Ops:
  0.0 0.7 copy-start
  0.7 0.7 copy-start.1
  1.4 0.7 copy-start.2
